TPU v7x, 32 devices: a whole 2x2x4 slice. The times are simulated.
32 devices in a mesh: seq: 8 (over z, x), head: 4 (over y, core).
Axes of the slice: x: 2, y: 2, z: 4, core: 2. Of those that a mesh axis runs over, the one named last changes fastest.
Arguments:
- query: bfloat16 [2048, 1024], P('seq', 'head'), may hold values from -20 to 20
- key_states: bfloat16 [2048, 1024], P('seq', 'head'), may hold values from -20 to 20
- values: bfloat16 [2048, 1024], P('seq', 'head'), may hold values from -6 to 6
- grad_out: bfloat16 [2048, 1024], P('seq', 'head'), may hold values from -6 to 6
- rand_blocks: int32 [32, 2], replicated, may hold values from 0 to 31, as said below
- global_blocks: int32 [2], replicated, may hold values from 0 to 31, as said below
Outputs:
- out: bfloat16 [2048, 1024], P('seq', 'head')
- dq: bfloat16 [2048, 1024], P('seq', 'head')
- dk: bfloat16 [2048, 1024], P('seq', 'head')
- dv: bfloat16 [2048, 1024], P('seq', 'head')
Inputs may be any that keep to these rules, and one draw needn't show every extreme that they name: `rand_blocks`: take the query blocks of one index of seq (aligned runs of 4 rows). Among their 8 entries at most 2 lie in the blocks of any one index o (blocks o*4 to o*4 + 3), and for every run some index receives exactly 2 of them. `global_blocks`: 2 different block numbers; the last of them is the sequence's last block.
All inputs are finite; a program needn't handle non-finite values.
Results may differ from a plain program's by a relative error of at most 0.04.
Values may be sent and summed in bfloat16 or wider, within the bound.
A program may use at most 128 MiB of HBM per device.

v0:
```python
import math

import jax
import jax.numpy as jnp
from jax import lax
from jax.sharding import PartitionSpec as P

HEAD_SIZE = 128
BLOCK_TOKENS = 64


def extended_2(block, sides, width):
    for axis, dim in sides:
        count = lax.axis_size(axis)
        forward = [(i, i + 1) for i in range(count - 1)]
        forward.append((count - 1, 0))
        backward = [(target, source) for source, target in forward]
        low = lax.ppermute(
            lax.slice_in_dim(block, block.shape[dim] - width, None, axis=dim), axis, forward
        )
        high = lax.ppermute(lax.slice_in_dim(block, 0, width, axis=dim), axis, backward)
        block = jnp.concatenate([low, block, high], axis=dim)
    return block


def shards(query, key_states, values, grad_out, rand_blocks, global_blocks):
    tokens, feature_width = query.shape
    head_count = feature_width // HEAD_SIZE
    nshard = lax.axis_size("seq")
    myself = lax.axis_index("seq")
    block_count = tokens // BLOCK_TOKENS
    nrand = rand_blocks.shape[1]
    nglob = global_blocks.shape[0]
    nfixed = 3 + nglob
    needed = block_count * nrand
    slots = max(2, (needed + nshard - 1) // nshard)
    double_width = 2 * feature_width
    score_scale = 1.0 / math.sqrt(HEAD_SIZE)
    paired = jnp.concatenate([key_states, values], axis=1)
    paired_blocks = paired.reshape(block_count, BLOCK_TOKENS, double_width)
    extended = extended_2(paired, (("seq", 0),), BLOCK_TOKENS)
    owners_glob = global_blocks // block_count
    local_glob = global_blocks % block_count
    pieces = []
    for glob_index in range(nglob):
        piece = lax.dynamic_slice_in_dim(
            paired, local_glob[glob_index] * BLOCK_TOKENS, BLOCK_TOKENS, 0
        )
        pieces.append(jnp.where(owners_glob[glob_index] == myself, piece.astype(jnp.float32), 0.0))
    global_rows = lax.psum(jnp.concatenate(pieces, axis=0), "seq").astype(jnp.bfloat16)
    table = rand_blocks.reshape(nshard, needed)
    owner_table = table // block_count
    local_table = table % block_count
    position = jnp.arange(needed)
    earlier_same = (owner_table[:, :, None] == owner_table[:, None, :]) & (
        position[None, None, :] < position[None, :, None]
    )
    rank_table = jnp.sum(earlier_same.astype(jnp.int32), axis=2)
    slot_range = jnp.arange(slots)
    matched = (owner_table[:, :, None] == myself) & (
        rank_table[:, :, None] == slot_range[None, None, :]
    )
    valid = jnp.any(matched, axis=1)
    send_local = jnp.sum(jnp.where(matched, local_table[:, :, None], 0), axis=1)
    outgoing = jnp.where(
        valid[:, :, None, None], paired_blocks[send_local], jnp.zeros((), jnp.bfloat16)
    )
    incoming = lax.all_to_all(outgoing, "seq", split_axis=0, concat_axis=0, tiled=True)
    my_owner = lax.dynamic_index_in_dim(owner_table, myself, 0, keepdims=False)
    my_rank = lax.dynamic_index_in_dim(rank_table, myself, 0, keepdims=False)
    flat_slot = my_owner * slots + my_rank
    fetched = incoming.reshape(nshard * slots, BLOCK_TOKENS, double_width)[flat_slot].reshape(
        block_count, nrand, BLOCK_TOKENS, double_width
    )
    ext_blocks = extended.reshape(block_count + 2, BLOCK_TOKENS, double_width)
    window_blocks = jnp.stack([ext_blocks[:-2], ext_blocks[1:-1], ext_blocks[2:]], axis=1)
    glob_wide = jnp.broadcast_to(
        global_rows.reshape(1, nglob, BLOCK_TOKENS, double_width),
        (block_count, nglob, BLOCK_TOKENS, double_width),
    )
    gathered = jnp.concatenate([window_blocks, glob_wide, fetched], axis=1)
    key_count = gathered.shape[1]
    key_matrix = gathered[..., :feature_width].reshape(
        block_count, key_count * BLOCK_TOKENS, head_count, HEAD_SIZE
    )
    value_matrix = gathered[..., feature_width:].reshape(
        block_count, key_count * BLOCK_TOKENS, head_count, HEAD_SIZE
    )
    query_matrix = query.reshape(block_count, BLOCK_TOKENS, head_count, HEAD_SIZE)
    logit_scores = (
        jnp.einsum("bqhd,bkhd->bhqk", query_matrix, key_matrix, preferred_element_type=jnp.float32)
        * score_scale
    )
    top = jnp.max(logit_scores, axis=-1, keepdims=True)
    lse = top + jnp.log(jnp.sum(jnp.exp(logit_scores - top), axis=-1, keepdims=True))
    probs = jnp.exp(logit_scores - lse)
    softmax_weights = probs.astype(jnp.bfloat16)
    attended_output = jnp.einsum(
        "bhqk,bkhd->bqhd", softmax_weights, value_matrix, preferred_element_type=jnp.float32
    ).astype(jnp.bfloat16)
    out = attended_output.reshape(tokens, feature_width)
    gradient_rows = grad_out.reshape(block_count, BLOCK_TOKENS, head_count, HEAD_SIZE)
    delta = jnp.sum(gradient_rows.astype(jnp.float32) * attended_output.astype(jnp.float32), axis=3)
    delta = jnp.transpose(delta, (0, 2, 1))[..., None]
    probability_gradient = jnp.einsum(
        "bqhd,bkhd->bhqk", gradient_rows, value_matrix, preferred_element_type=jnp.float32
    )
    dscore = (probs * (probability_gradient - delta) * score_scale).astype(jnp.bfloat16)
    query_gradient = jnp.einsum(
        "bhqk,bkhd->bqhd", dscore, key_matrix, preferred_element_type=jnp.float32
    ).astype(jnp.bfloat16)
    query_gradient = query_gradient.reshape(tokens, feature_width)
    key_term = jnp.einsum(
        "bhqk,bqhd->bkhd", dscore, query_matrix, preferred_element_type=jnp.float32
    )
    value_term = jnp.einsum(
        "bhqk,bqhd->bkhd", softmax_weights, gradient_rows, preferred_element_type=jnp.float32
    )
    terms = jnp.concatenate(
        [
            key_term.reshape(block_count, key_count, BLOCK_TOKENS, feature_width),
            value_term.reshape(block_count, key_count, BLOCK_TOKENS, feature_width),
        ],
        axis=3,
    )
    zero_one = jnp.zeros((1, BLOCK_TOKENS, double_width), jnp.float32)
    zero_two = jnp.zeros((2, BLOCK_TOKENS, double_width), jnp.float32)
    ext_grad = (
        jnp.concatenate([terms[:, 0], zero_two], axis=0)
        + jnp.concatenate([zero_one, terms[:, 1], zero_one], axis=0)
        + jnp.concatenate([zero_two, terms[:, 2]], axis=0)
    )
    rims = jnp.concatenate([ext_grad[0], ext_grad[-1]], axis=0)
    returned = extended_2(rims, (("seq", 0),), BLOCK_TOKENS)
    own = ext_grad[1:-1]
    own = own.at[0].add(returned[:BLOCK_TOKENS]).at[-1].add(returned[3 * BLOCK_TOKENS :])
    glob_terms = jnp.sum(terms[:, 3:nfixed], axis=0)
    glob_total = lax.psum(glob_terms, "seq")
    block_ids = jnp.arange(block_count)
    for glob_index in range(nglob):
        owned_here = (block_ids == local_glob[glob_index]) & (owners_glob[glob_index] == myself)
        own = own + jnp.where(owned_here[:, None, None], glob_total[glob_index][None], 0.0)
    tile_terms = terms[:, nfixed:].reshape(needed, BLOCK_TOKENS, double_width).astype(jnp.bfloat16)
    empty = jnp.zeros((nshard * slots,) + tile_terms.shape[1:], tile_terms.dtype)
    arrived = lax.all_to_all(
        empty.at[flat_slot].set(tile_terms).reshape((nshard, slots) + tile_terms.shape[1:]),
        "seq",
        split_axis=0,
        concat_axis=0,
        tiled=True,
    )
    selector = (send_local.reshape(-1)[None, :] == block_ids[:, None]) & valid.reshape(-1)[None, :]
    own = own + jnp.einsum(
        "bs,sqc->bqc",
        selector.astype(jnp.bfloat16),
        arrived.reshape(nshard * slots, BLOCK_TOKENS, double_width),
        preferred_element_type=jnp.float32,
    )
    own = own.reshape(tokens, double_width)
    dkey = own[:, :feature_width].astype(jnp.bfloat16)
    dvalue = own[:, feature_width:].astype(jnp.bfloat16)
    return (out, query_gradient, dkey, dvalue)


def solution(mesh):
    in_specs = (P("seq", "head"), P("seq", "head"), P("seq", "head"), P("seq", "head"), P(), P())
    out_specs = (P("seq", "head"), P("seq", "head"), P("seq", "head"), P("seq", "head"))
    return jax.shard_map(shards, mesh=mesh, in_specs=in_specs, out_specs=out_specs, check_vma=False)
```

profile of v0, /device:TPU:0, one launch (start us, length us, event | category | flops | bytes accessed | tf_op | source)
XLA Modules:
  0.0 201.1 jit_solution(15153234952446303233)
XLA Ops:
  7.2 0.9 constant_dynamic-update-slice_fusion.1
  8.1 0.8 copy.73
  9.8 0.9 constant_dynamic-update-slice_fusion
  10.7 0.6 gather_fusion
  11.4 1.1 broadcast_select_fusion
  12.5 7.4 %all-to-all-start = ((bf16[8,2,64,512]{3,2,1,0:T(8,128)(2,1)}), bf16[8,2,64,512]{3,2,1,0:T(8,128)(2,1)S(1)}, u32[]{:S(2)}, u32[]{:S(2)}) async-start(bf16[8,2,64,512]{3,2,1,0:T(8,128)(2,1)} %broadcast_select_fusion), calls=%async_computation | async-start | bytes 2097152 | tf_op jit(solution)/shard_map/all_to_all | solution.py:68
  19.9 4.8 %collective-permute-start.1 = (bf16[64,512]{1,0:T(8,128)(2,1)S(1)}, bf16[64,512]{1,0:T(8,128)(2,1)S(1)}, u32[]{:S(2)}, u32[]{:S(2)}) collective-permute-start(bf16[64,512]{1,0:T(8,128)(2,1)S(1)} %get-tuple-element.45), channel_id=1, source_target_pairs={{4,0},{8,4},{12,8},{16,12},{20,16},{24,20},{28,24},{0,28},{5,1},{9... | collective-permute-start | bytes 196616 | tf_op jit(solution)/shard_map/ppermute | solution.py:21
  24.7 0.6 fusion.46
  28.3 45.0 %all-reduce.6 = bf16[128,512]{1,0:T(8,128)(2,1)S(1)} all-reduce(f32[128,512]{1,0:T(8,128)S(1)} %pad_maximum_fusion.3), channel_id=1, replica_groups=mesh['seq'=8,'head'=4] {'seq'}, use_global_device_ids=true, to_apply=%region_0.1 | all-reduce | flops 65536 | bytes 393216 | tf_op jit(solution)/shard_map/psum | solution.py:50
  73.5 0.8 constant_dynamic-update-slice_fusion.5
  74.2 0.7 constant_dynamic-update-slice_fusion.4
  75.0 0.7 constant_dynamic-update-slice_fusion.3
  75.7 0.8 broadcast_dynamic-update-slice_fusion
  76.5 0.6 gather_fusion.1
  77.1 0.9 constant_dynamic-update-slice_fusion.2
  78.0 1.6 fusion.43
  79.6 1.1 reshape.302
  80.9 0.6 fusion.48
  81.9 0.7 convolution_bitcast_fusion
  82.7 1.1 multiply_reduce_fusion
  83.8 0.5 fusion.4
  84.3 2.7 %copy.91 = f32[4,448,2,128]{3,2,1,0:T(2,128)} copy(f32[4,448,2,128]{3,1,2,0:T(8,128)S(1)} %convolution_bitcast_fusion) | data formatting | bytes 3670016 | tf_op jit(solution)/shard_map/bhqk,bqhd->bkhd/transpose | solution.py:116
  87.0 2.7 %reshape.309 = f32[4,7,64,256]{3,2,1,0:T(8,128)S(1)} reshape(f32[4,448,2,128]{3,2,1,0:T(2,128)} %copy.91) | data formatting | bytes 3670016 | tf_op jit(solution)/shard_map/reshape | solution.py:122
  90.2 2.7 %copy.89 = f32[4,448,2,128]{3,2,1,0:T(2,128)} copy(f32[4,448,2,128]{3,1,2,0:T(8,128)S(1)} %convolution_bitcast_fusion.1) | data formatting | bytes 3670016 | tf_op jit(solution)/shard_map/bhqk,bqhd->bkhd/transpose | solution.py:113
  92.9 3.6 %reshape.308 = f32[4,7,64,256]{3,2,1,0:T(8,128)} reshape(f32[4,448,2,128]{3,2,1,0:T(2,128)} %copy.89) | data formatting | bytes 3670016 | tf_op jit(solution)/shard_map/reshape | solution.py:121
  96.5 2.0 pad_maximum_fusion
  98.5 1.8 copy-done
  100.6 0.8 scatter_fusion
  101.4 2.1 %copy.99 = bf16[8,2,64,512]{3,1,2,0:T(2,128)(2,1)} copy(bf16[8,2,64,512]{3,2,1,0:T(8,128)(2,1)S(1)} %bitcast.105) | data formatting | bytes 2097152 | tf_op jit(solution)/shard_map/reshape | solution.py:146
  103.4 4.5 %all-to-all-start.1 = ((bf16[8,2,64,512]{3,1,2,0:T(2,128)(2,1)}), bf16[8,2,64,512]{3,1,2,0:T(2,128)(2,1)S(1)}, u32[]{:S(2)}, u32[]{:S(2)}) async-start(bf16[8,2,64,512]{3,1,2,0:T(2,128)(2,1)} %copy.99), calls=%async_computation.1 | async-start | bytes 2097152 | tf_op jit(solution)/shard_map/all_to_all | solution.py:145
  108.2 0.7 compare_and_fusion
  108.8 0.7 compare_and_fusion.1
  109.5 1.6 fusion.42
  111.2 0.6 copy-done.2
  111.9 0.7 fusion.17
  112.5 1.8 collective-permute-start.2
  114.3 2.0 %copy_reduce_fusion = f32[2,64,512]{2,1,0:T(8,128)} fusion(f32[4,7,64,512]{3,2,1,0:T(8,128)} %copy-done), kind=kLoop, calls=%fused_computation.18 | loop fusion | flops 196608 | bytes 1310720 | tf_op jit(solution)/shard_map/reduce_sum | solution.py:137
  116.4 1.4 fusion.6
  117.8 1.2 fusion.12
  119.2 0.7 copy.146
  120.0 0.7 copy.145
  120.7 7.4 %collective-permute-done.2 = f32[64,512]{1,0:T(8,128)} collective-permute-done((f32[64,512]{1,0:T(8,128)}, f32[64,512]{1,0:T(8,128)}, u32[]{:S(2)}, u32[]{:S(2)}) %collective-permute-start.2) | collective-permute-done | bytes 131104 | tf_op jit(solution)/shard_map/ppermute | solution.py:18
  128.1 1.0 fusion.21
  129.5 59.6 %all-reduce.5.cloned.1.call-done = f32[2,64,512]{2,1,0:T(8,128)} async-done(((f32[2,64,512]{2,1,0:T(8,128)}), f32[2,64,512]{2,1,0:T(8,128)}) %all-reduce.5.cloned.1.call-update) | async-done | bytes 262160 | tf_op jit(solution)/shard_map/psum | solution.py:138
  189.0 1.0 slice_bitcast_fusion.1
  190.2 1.3 scatter-add.9
  191.5 1.1 copy.100
  193.6 0.7 fusion.44
  (69 shorter events, 5.0 us)
Async XLA Ops:
  11.4 13.3 %copy-start.8 = (s32[2]{0:T(128)S(1)}, s32[2]{0:T(128)}, u32[]{:S(2)}) copy-start(s32[2]{0:T(128)} %param.15) | copy-start | bytes 28
  11.4 15.4 %copy-start.6 = (bf16[256,256]{1,0:T(8,128)(2,1)S(1)}, bf16[256,256]{1,0:T(8,128)(2,1)}, u32[]{:S(2)}) copy-start(bf16[256,256]{1,0:T(8,128)(2,1)} %param.13) | copy-start | bytes 393220
  12.5 15.7 %copy-start.7 = (bf16[256,256]{1,0:T(8,128)(2,1)S(1)}, bf16[256,256]{1,0:T(8,128)(2,1)}, u32[]{:S(2)}) copy-start(bf16[256,256]{1,0:T(8,128)(2,1)} %param.10) | copy-start | bytes 393220
  12.5 64.0 %all-to-all-start = ((bf16[8,2,64,512]{3,2,1,0:T(8,128)(2,1)}), bf16[8,2,64,512]{3,2,1,0:T(8,128)(2,1)S(1)}, u32[]{:S(2)}, u32[]{:S(2)}) async-start(bf16[8,2,64,512]{3,2,1,0:T(8,128)(2,1)} %broadcast_select_fusion), calls=%async_computation | async-start | bytes 2097152 | tf_op jit(solution)/shard_map/all_to_all | solution.py:68
  19.9 53.5 %collective-permute-start.1 = (bf16[64,512]{1,0:T(8,128)(2,1)S(1)}, bf16[64,512]{1,0:T(8,128)(2,1)S(1)}, u32[]{:S(2)}, u32[]{:S(2)}) collective-permute-start(bf16[64,512]{1,0:T(8,128)(2,1)S(1)} %get-tuple-element.45), channel_id=1, source_target_pairs={{4,0},{8,4},{12,8},{16,12},{20,16},{24,20},{28,24},{0,28},{5,1},{9... | collective-permute-start | bytes 196616 | tf_op jit(solution)/shard_map/ppermute | solution.py:21
  24.7 48.7 %collective-permute-start = (bf16[64,512]{1,0:T(8,128)(2,1)S(1)}, bf16[64,512]{1,0:T(8,128)(2,1)S(1)}, u32[]{:S(2)}, u32[]{:S(2)}) collective-permute-start(bf16[64,512]{1,0:T(8,128)(2,1)S(1)} %get-tuple-element.46), channel_id=1, source_target_pairs={{0,4},{4,8},{8,12},{12,16},{16,20},{20,24},{24,28},{28,0},{1,5},{5... | collective-permute-start | bytes 196616 | tf_op jit(solution)/shard_map/ppermute | solution.py:18
  81.5 1.2 copy-start.1
  84.3 5.4 %copy-start.4 = (bf16[4,2,64,448]{3,2,1,0:T(8,128)(2,1)}, bf16[4,2,64,448]{3,2,1,0:T(8,128)(2,1)S(1)}, u32[]{:S(2)}) copy-start(bf16[4,2,64,448]{3,2,1,0:T(8,128)(2,1)S(1)} %fusion.4) | copy-start | bytes 1376260
  98.5 1.8 copy-start
  103.4 88.1 %all-to-all-start.1 = ((bf16[8,2,64,512]{3,1,2,0:T(2,128)(2,1)}), bf16[8,2,64,512]{3,1,2,0:T(2,128)(2,1)S(1)}, u32[]{:S(2)}, u32[]{:S(2)}) async-start(bf16[8,2,64,512]{3,1,2,0:T(2,128)(2,1)} %copy.99), calls=%async_computation.1 | async-start | bytes 2097152 | tf_op jit(solution)/shard_map/all_to_all | solution.py:145
  107.9 81.1 %all-reduce.5.cloned.1.call-start = ((), (), s32[]{:S(2)}) async-start(), calls=%async_computation.2 | async-start | bytes 524288 | tf_op jit(solution)/shard_map/psum | solution.py:138
  111.2 0.7 copy-start.2
  112.5 15.6 %collective-permute-start.2 = (f32[64,512]{1,0:T(8,128)}, f32[64,512]{1,0:T(8,128)}, u32[]{:S(2)}, u32[]{:S(2)}) collective-permute-start(f32[64,512]{1,0:T(8,128)} %fusion.17), channel_id=1, source_target_pairs={{0,4},{4,8},{8,12},{12,16},{16,20},{20,24},{24,28},{28,0},{1,5},{5... | collective-permute-start | bytes 393224 | tf_op jit(solution)/shard_map/ppermute | solution.py:18
  116.4 2.7 %copy-start.5 = (bf16[4,64,2,128]{3,1,2,0:T(8,128)(2,1)S(1)}, bf16[4,64,2,128]{3,1,2,0:T(8,128)(2,1)}, u32[]{:S(2)}) copy-start(bf16[4,64,2,128]{3,1,2,0:T(8,128)(2,1)} %get-tuple-element.56) | copy-start | bytes 393220
  117.8 10.3 %copy-start.3 = (f32[1,64,512]{2,1,0:T(8,128)S(1)}, f32[1,64,512]{2,1,0:T(8,128)}, u32[]{:S(2)}) copy-start(f32[1,64,512]{2,1,0:T(8,128)} %copy-done.2) | copy-start | bytes 393220
  129.4 60.6 %collective-permute-start.3 = (f32[64,512]{1,0:T(8,128)S(1)}, f32[64,512]{1,0:T(8,128)S(1)}, u32[]{:S(2)}, u32[]{:S(2)}) collective-permute-start(f32[64,512]{1,0:T(8,128)S(1)} %get-tuple-element.35), channel_id=1, source_target_pairs={{4,0},{8,4},{12,8},{16,12},{20,16},{24,20},{28,24},{0,28},{5,1},{9... | collective-permute-start | bytes 393224 | tf_op jit(solution)/shard_map/ppermute | solution.py:21
Sparse Core Ops, SparseCore 0:
  116.5 72.4 all-reduce.4
where the time goes:
time: 202 us; the launch traced here: 201 us
  waiting for transfers between devices  67 us (33%)
  blocking collectives  45 us (22%)
  local copies, waits for them, and re-layouts  37.5 us (19%)
  starting transfers between devices  18.8 us (9%)
  between operations  17.1 us (8%)
  other arithmetic  10.5 us (5%)
  matrix products  5.15 us (3%)
    psum x1, waiting for transfers between devices, shards(): glob_total = lax.psum(glob_terms, 'seq')  59.6 us
    psum x1, blocking collectives, shards(): lax.psum(jnp.concatenate(pieces, axis=0), 'seq').astype(jnp.bfloat16)  45 us
    unnamed x30, local copies, waits for them, and re-layouts  8.83 us
    all_to_all x1, starting transfers between devices, shards(): lax.all_to_all(outgoing, 'seq', split_axis=0, concat_axis=0, tiled=True)  7.38 us
    ppermute x2, waiting for transfers between devices, extended_2(): lax.ppermute(lax.slice_in_dim(block, block.shape[dim] - width, None, axis...  7.38 us
    ppermute x2, starting transfers between devices, extended_2(): lax.ppermute(lax.slice_in_dim(block, 0, width, axis=dim), axis, backward)  4.83 us
    all_to_all x1, starting transfers between devices, shards(): lax.all_to_all(empty.at[flat_slot].set(tile_terms).reshape((nshard, slots...  4.53 us
  transfers between devices with their start and end apart: 7, of which 2 were waited for; matrix products, arithmetic and copies ran while one was open for 9% of the time, Pallas kernels for 0%

commit v1 on v0

--- a/solution.py
+++ b/solution.py
@@ -3,6 +3,8 @@
 import jax
 import jax.numpy as jnp
 from jax import lax
+from jax.experimental import pallas as pl
+from jax.experimental.pallas import tpu as pltpu
 from jax.sharding import PartitionSpec as P
 
 HEAD_SIZE = 128
@@ -21,6 +23,14 @@
         high = lax.ppermute(lax.slice_in_dim(block, 0, width, axis=dim), axis, backward)
         block = jnp.concatenate([low, block, high], axis=dim)
     return block
+
+
+def pick_blocks(blocks, index):
+    onehot = (index[..., None] == jnp.arange(blocks.shape[0])).astype(blocks.dtype)
+    picked = jnp.einsum(
+        "...b,bqc->...qc", onehot, blocks, preferred_element_type=jnp.float32
+    )
+    return picked.astype(blocks.dtype)
 
 
 def shards(query, key_states, values, grad_out, rand_blocks, global_blocks):
@@ -63,15 +73,15 @@
     valid = jnp.any(matched, axis=1)
     send_local = jnp.sum(jnp.where(matched, local_table[:, :, None], 0), axis=1)
     outgoing = jnp.where(
-        valid[:, :, None, None], paired_blocks[send_local], jnp.zeros((), jnp.bfloat16)
+        valid[:, :, None, None], pick_blocks(paired_blocks, send_local), jnp.zeros((), jnp.bfloat16)
     )
     incoming = lax.all_to_all(outgoing, "seq", split_axis=0, concat_axis=0, tiled=True)
     my_owner = lax.dynamic_index_in_dim(owner_table, myself, 0, keepdims=False)
     my_rank = lax.dynamic_index_in_dim(rank_table, myself, 0, keepdims=False)
     flat_slot = my_owner * slots + my_rank
-    fetched = incoming.reshape(nshard * slots, BLOCK_TOKENS, double_width)[flat_slot].reshape(
-        block_count, nrand, BLOCK_TOKENS, double_width
-    )
+    fetched = pick_blocks(
+        incoming.reshape(nshard * slots, BLOCK_TOKENS, double_width), flat_slot
+    ).reshape(block_count, nrand, BLOCK_TOKENS, double_width)
     ext_blocks = extended.reshape(block_count + 2, BLOCK_TOKENS, double_width)
     window_blocks = jnp.stack([ext_blocks[:-2], ext_blocks[1:-1], ext_blocks[2:]], axis=1)
     glob_wide = jnp.broadcast_to(
@@ -162,7 +172,349 @@
     return (out, query_gradient, dkey, dvalue)
 
 
+PAIRS = 4
+SIDE = 2 * HEAD_SIZE
+MASKED = -1e30
+NT = (((1,), (1,)), ((), ()))
+TN = (((0,), (0,)), ((), ()))
+NN = (((1,), (0,)), ((), ()))
+
+
+def dot(a, b, dims):
+    return lax.dot_general(a, b, dims, preferred_element_type=jnp.float32)
+
+
+def fused_kernel(
+    rand_ref, glob_ref, q_ref, k_ref, v_ref, g_ref,
+    o_ref, dq_ref, dk_ref, dv_ref,
+    kv, qg, pack, bias, score, dprob, top, total, acc_out, acc_dq,
+    part, send, from_near, from_far, swap_out, swap_in,
+    far_sent, near_sent, kv_got, grad_sent, near_got, far_got, swap_sent, swap_got,
+):
+    tokens = q_ref.shape[0]
+    rows = 2 * tokens
+    blocks = tokens // BLOCK_TOKENS
+    nrand = rand_ref.shape[1]
+    nglob = glob_ref.shape[0]
+    block_total = rand_ref.shape[0]
+    scale = 1.0 / math.sqrt(HEAD_SIZE)
+    scale2 = scale * math.log2(math.e)
+
+    s = lax.axis_index("seq")
+    z, x = s // 2, s % 2
+    partner = s + 1 - 2 * x
+    m = z // 2
+    w = z + m * (3 - 2 * z)
+    step = 1 - 2 * m
+    far = 2 * (z + step) + x
+    near = 2 * (z - step) + x
+
+    def slot_of(k, other):
+        return 2 * (k + m * (3 - 2 * k)) + x + other * (1 - 2 * x)
+
+    def remote(src, dst, sent, got, to):
+        return pltpu.make_async_remote_copy(
+            src_ref=src, dst_ref=dst, send_sem=sent, recv_sem=got,
+            device_id={"seq": to}, device_id_type=pl.DeviceIdType.MESH,
+        )
+
+    def kv_far(slot):
+        return remote(kv.at[slot], kv.at[slot], far_sent.at[slot], kv_got.at[slot], far)
+
+    def kv_near(slot):
+        return remote(kv.at[slot], kv.at[slot], near_sent.at[slot], kv_got.at[slot], near)
+
+    kv_swap = remote(pack.at[0], kv.at[s], swap_sent.at[0], kv_got.at[s], partner)
+    kv_swapped = remote(pack.at[0], kv.at[partner], swap_sent.at[0], kv_got.at[partner], partner)
+    qg_swap = remote(pack.at[1], qg.at[x], swap_sent.at[1], swap_got.at[0], partner)
+    oq_swap = remote(swap_out.at[0], swap_in.at[0], swap_sent.at[2], swap_got.at[1], partner)
+    kg_swap = remote(swap_out.at[1], swap_in.at[1], swap_sent.at[3], swap_got.at[2], partner)
+
+    barrier = pltpu.get_barrier_semaphore()
+    for to in (partner, far):
+        pl.semaphore_signal(
+            barrier, inc=1, device_id={"seq": to}, device_id_type=pl.DeviceIdType.MESH
+        )
+
+    @pl.when(w == 1)
+    def _():
+        pl.semaphore_signal(
+            barrier, inc=1, device_id={"seq": near}, device_id_type=pl.DeviceIdType.MESH
+        )
+
+    mine = pl.ds(pl.multiple_of(x * HEAD_SIZE, HEAD_SIZE), HEAD_SIZE)
+    theirs = pl.ds(pl.multiple_of((1 - x) * HEAD_SIZE, HEAD_SIZE), HEAD_SIZE)
+    kv[s, :, :HEAD_SIZE] = k_ref[:, mine]
+    kv[s, :, HEAD_SIZE:] = v_ref[:, mine]
+    pack[0, :, :HEAD_SIZE] = k_ref[:, theirs]
+    pack[0, :, HEAD_SIZE:] = v_ref[:, theirs]
+    qg[x, :, :HEAD_SIZE] = q_ref[:, mine]
+    qg[x, :, HEAD_SIZE:] = g_ref[:, mine]
+    pack[1, :, :HEAD_SIZE] = q_ref[:, theirs]
+    pack[1, :, HEAD_SIZE:] = g_ref[:, theirs]
+
+    pl.semaphore_wait(barrier, 2 + w)
+    kv_swap.start()
+    kv_far(s).start()
+
+    @pl.when(w == 1)
+    def _():
+        kv_near(s).start()
+
+    qg_swap.start()
+
+    lane_block = lax.broadcasted_iota(jnp.int32, (1, rows), 1) // BLOCK_TOKENS
+    first = z * 2 * blocks
+    block = first + lane_block
+    entries = [
+        jnp.where(block == 0, block_total - 1, block - 1),
+        block,
+        jnp.where(block == block_total - 1, 0, block + 1),
+    ]
+    for j in range(nglob):
+        entries.append(jnp.full((1, rows), glob_ref[j], jnp.int32))
+    for j in range(nrand):
+        entry = jnp.zeros((1, rows), jnp.int32)
+        for i in range(2 * blocks):
+            entry = jnp.where(lane_block == i, rand_ref[first + i, j], entry)
+        entries.append(entry)
+    key_block = lax.broadcasted_iota(jnp.int32, (block_total, rows), 0)
+    count = jnp.zeros((block_total, rows), jnp.float32)
+    for entry in entries:
+        count = count + jnp.where(key_block == entry, 1.0, 0.0)
+    bias_all = jnp.where(count > 0.0, jnp.log2(jnp.maximum(count, 1.0)), MASKED)
+    for j in range(2 * PAIRS):
+        bias[j] = bias_all[j * blocks : (j + 1) * blocks]
+
+    top[...] = jnp.full_like(top, MASKED)
+    total[...] = jnp.zeros_like(total)
+    acc_out[...] = jnp.zeros_like(acc_out)
+    acc_dq[...] = jnp.zeros_like(acc_dq)
+
+    kv_swapped.wait_recv()
+    kv_far(partner).start()
+
+    @pl.when(w == 1)
+    def _():
+        kv_near(partner).start()
+
+    qg_swap.wait_recv()
+
+    def queries():
+        return qg[:, :, :HEAD_SIZE].reshape(rows, HEAD_SIZE)
+
+    def grads():
+        return qg[:, :, HEAD_SIZE:].reshape(rows, HEAD_SIZE)
+
+    def forward(slot):
+        key = kv[slot, :, :HEAD_SIZE]
+        value = kv[slot, :, HEAD_SIZE:]
+        st = dot(key, queries(), NT) * scale2
+        st = (st.reshape(blocks, BLOCK_TOKENS, rows) + bias[slot][:, None, :]).reshape(tokens, rows)
+        score[slot] = st
+        old = top[...]
+        new = jnp.maximum(old, jnp.max(st, axis=0, keepdims=True))
+        e = jnp.exp2(st - new)
+        alpha = jnp.exp2(old - new)
+        top[...] = new
+        total[...] = total[...] * alpha + jnp.sum(e, axis=0, keepdims=True)
+        acc_out[...] = acc_out[...] * alpha + dot(value, e.astype(jnp.bfloat16), TN)
+        dprob[slot] = dot(value, grads(), NT)
+
+    @pl.loop(0, 2)
+    def _(i):
+        forward(s + i * (1 - 2 * x))
+
+    @pl.loop(0, 6)
+    def _(i):
+        k_end = 1 + i // 2
+        o_end = i % 2
+        k_mid = jnp.where(i < 4, (i % 2) * 2, 3)
+        o_mid = jnp.where(i < 4, i // 2, i % 2)
+        k = jnp.where(w == 0, k_end, k_mid)
+        slot = slot_of(k, jnp.where(w == 0, o_end, o_mid))
+        kv_far(slot).wait_recv()
+
+        @pl.when((w == 1) & (k == 0))
+        def _():
+            kv_far(slot).start()
+
+        @pl.when((w == 1) & (k > 0))
+        def _():
+            kv_near(slot).start()
+
+        forward(slot)
+
+    lse = top[...] + jnp.log2(total[...])
+    out_t = (acc_out[...] / total[...]).astype(jnp.bfloat16).astype(jnp.float32)
+    grad_t = grads().astype(jnp.float32).T
+    delta = jnp.sum(out_t * grad_t, axis=0, keepdims=True)
+    acc_out[...] = out_t
+    top[...] = lse
+    total[...] = delta
+
+    def grad_send(slot, to, got, sem):
+        return remote(send.at[slot], got.at[slot], grad_sent.at[slot], sem.at[slot], to)
+
+    @pl.loop(0, 8)
+    def _(i):
+        k_low = jnp.where(w == 0, 3 - i // 2, i // 2 - 2)
+        k = jnp.where(i < 4, 3 - i // 2, k_low)
+        slot = slot_of(k, 1 - i % 2)
+        prob = jnp.exp2(score[slot] - top[...])
+        ds = (prob * (dprob[slot] - total[...]) * scale).astype(jnp.bfloat16)
+        dk_term = dot(ds, queries(), NN)
+        dv_term = dot(prob.astype(jnp.bfloat16), grads(), NN)
+        is_sent = (w == 0) & (i < 6)
+
+        @pl.when(is_sent)
+        def _():
+            send[slot, :, :HEAD_SIZE] = dk_term.astype(jnp.bfloat16)
+            send[slot, :, HEAD_SIZE:] = dv_term.astype(jnp.bfloat16)
+            grad_send(slot, far, from_near, near_got).start()
+
+        @pl.when(jnp.logical_not(is_sent))
+        def _():
+            part[slot, :, :HEAD_SIZE] = dk_term
+            part[slot, :, HEAD_SIZE:] = dv_term
+
+        acc_dq[...] += dot(kv[slot, :, :HEAD_SIZE], ds, TN)
+
+    out_rows = acc_out[...].T.astype(jnp.bfloat16)
+    dq_rows = acc_dq[...].T.astype(jnp.bfloat16)
+    low_o, high_o = out_rows[:tokens], out_rows[tokens:]
+    low_q, high_q = dq_rows[:tokens], dq_rows[tokens:]
+
+    @pl.when(x == 0)
+    def _():
+        swap_out[0, :, :HEAD_SIZE] = high_o
+        swap_out[0, :, HEAD_SIZE:] = high_q
+        o_ref[:, :HEAD_SIZE] = low_o
+        dq_ref[:, :HEAD_SIZE] = low_q
+
+    @pl.when(x == 1)
+    def _():
+        swap_out[0, :, :HEAD_SIZE] = low_o
+        swap_out[0, :, HEAD_SIZE:] = low_q
+        o_ref[:, HEAD_SIZE:] = high_o
+        dq_ref[:, HEAD_SIZE:] = high_q
+
+    oq_swap.start()
+
+    @pl.when(w == 1)
+    def _():
+        for k, other in ((3, 1), (3, 0), (0, 1), (2, 1), (0, 0), (2, 0)):
+            slot = slot_of(k, other)
+            if k == 0:
+                grad_send(slot, far, from_far, far_got).wait_recv()
+                added = part[slot] + from_far[slot].astype(jnp.float32)
+                send[slot] = added.astype(jnp.bfloat16)
+                grad_send(slot, near, from_far, far_got).start()
+            else:
+                grad_send(slot, far, from_near, near_got).wait_recv()
+                added = part[slot] + from_near[slot].astype(jnp.float32)
+                send[slot] = added.astype(jnp.bfloat16)
+                grad_send(slot, far, from_far, far_got).start()
+
+    def finish(slot):
+        grad_send(slot, far, from_far, far_got).wait_recv()
+        part[slot] += from_far[slot].astype(jnp.float32)
+
+        @pl.when(w == 1)
+        def _():
+            grad_send(slot, far, from_near, near_got).wait_recv()
+            part[slot] += from_near[slot].astype(jnp.float32)
+
+    finish(partner)
+    swap_out[1] = part[partner].astype(jnp.bfloat16)
+    kg_swap.start()
+    finish(s)
+    dk_ref[:, mine] = part[s, :, :HEAD_SIZE].astype(jnp.bfloat16)
+    dv_ref[:, mine] = part[s, :, HEAD_SIZE:].astype(jnp.bfloat16)
+    oq_swap.wait_recv()
+    o_ref[:, theirs] = swap_in[0, :, :HEAD_SIZE]
+    dq_ref[:, theirs] = swap_in[0, :, HEAD_SIZE:]
+
+    kv_swap.wait_send()
+    qg_swap.wait_send()
+    oq_swap.wait_send()
+    for slot in (s, partner):
+        kv_far(slot).wait_send()
+
+    @pl.when(w == 0)
+    def _():
+        for k in (1, 2, 3):
+            for other in (0, 1):
+                grad_send(slot_of(k, other), far, from_near, near_got).wait_send()
+
+    @pl.when(w == 1)
+    def _():
+        for other in (0, 1):
+            kv_far(slot_of(0, other)).wait_send()
+            for k in (1, 2, 3):
+                kv_near(slot_of(k, other)).wait_send()
+            for k in (0, 2, 3):
+                grad_send(slot_of(k, other), far, from_far, far_got).wait_send()
+
+    kg_swap.wait_recv()
+    dk_ref[:, theirs] = swap_in[1, :, :HEAD_SIZE]
+    dv_ref[:, theirs] = swap_in[1, :, HEAD_SIZE:]
+    kg_swap.wait_send()
+
+
+def fused(query, key_states, values, grad_out, rand_blocks, global_blocks):
+    tokens = query.shape[0]
+    rows = 2 * tokens
+    slots = 2 * PAIRS
+    blocks = tokens // BLOCK_TOKENS
+    bf16, f32 = jnp.bfloat16, jnp.float32
+    vmem = pl.BlockSpec(memory_space=pltpu.VMEM)
+    smem = pl.BlockSpec(memory_space=pltpu.SMEM)
+    dma = pltpu.SemaphoreType.DMA
+    work = 6 * 2 * rows * slots * tokens * HEAD_SIZE
+    return pl.pallas_call(
+        fused_kernel,
+        out_shape=[jax.ShapeDtypeStruct(query.shape, bf16)] * 4,
+        in_specs=[smem, smem, vmem, vmem, vmem, vmem],
+        out_specs=[vmem] * 4,
+        scratch_shapes=[
+            pltpu.VMEM((slots, tokens, SIDE), bf16),
+            pltpu.VMEM((2, tokens, SIDE), bf16),
+            pltpu.VMEM((2, tokens, SIDE), bf16),
+            pltpu.VMEM((slots, blocks, rows), f32),
+            pltpu.VMEM((slots, tokens, rows), f32),
+            pltpu.VMEM((slots, tokens, rows), f32),
+            pltpu.VMEM((1, rows), f32),
+            pltpu.VMEM((1, rows), f32),
+            pltpu.VMEM((HEAD_SIZE, rows), f32),
+            pltpu.VMEM((HEAD_SIZE, rows), f32),
+            pltpu.VMEM((slots, tokens, SIDE), f32),
+            pltpu.VMEM((slots, tokens, SIDE), bf16),
+            pltpu.VMEM((slots, tokens, SIDE), bf16),
+            pltpu.VMEM((slots, tokens, SIDE), bf16),
+            pltpu.VMEM((2, tokens, SIDE), bf16),
+            pltpu.VMEM((2, tokens, SIDE), bf16),
+            dma((slots,)), dma((slots,)), dma((slots,)), dma((slots,)),
+            dma((slots,)), dma((slots,)), dma((4,)), dma((3,)),
+        ],
+        compiler_params=pltpu.CompilerParams(
+            collective_id=0, has_side_effects=True, vmem_limit_bytes=40 * 1024 * 1024
+        ),
+        cost_estimate=pl.CostEstimate(
+            flops=work, bytes_accessed=8 * tokens * SIDE * 2, transcendentals=2 * rows * slots * tokens
+        ),
+    )(rand_blocks, global_blocks, query, key_states, values, grad_out)
+
+
+def device_program(query, key_states, values, grad_out, rand_blocks, global_blocks):
+    if lax.axis_size("seq") == 2 * PAIRS and query.shape == (4 * BLOCK_TOKENS, 2 * HEAD_SIZE):
+        return tuple(fused(query, key_states, values, grad_out, rand_blocks, global_blocks))
+    return shards(query, key_states, values, grad_out, rand_blocks, global_blocks)
+
+
 def solution(mesh):
     in_specs = (P("seq", "head"), P("seq", "head"), P("seq", "head"), P("seq", "head"), P(), P())
     out_specs = (P("seq", "head"), P("seq", "head"), P("seq", "head"), P("seq", "head"))
-    return jax.shard_map(shards, mesh=mesh, in_specs=in_specs, out_specs=out_specs, check_vma=False)
+    return jax.shard_map(
+        device_program, mesh=mesh, in_specs=in_specs, out_specs=out_specs, check_vma=False
+    )

time: 202 us -> 53.8 us (0.27)
  waiting for transfers between devices: 67 us -> 0 us
  Pallas kernels: 0 us -> 45.9 us
  blocking collectives: 45 us -> 0 us
  local copies, waits for them, and re-layouts: 37.5 us -> 7.01 us
  starting transfers between devices: 18.8 us -> 0 us
  between operations: 17.1 us -> 0.65 us
  other arithmetic: 10.5 us -> 0 us
  matrix products: 5.15 us -> 0 us
    psum x1 -> x0, waiting for transfers between devices: 59.6 us -> none  [shards(): glob_total = lax.psum(glob_terms, 'seq')]
    pallas_call x0 -> x1, Pallas kernels: none -> 45.9 us  [fused(): pl.pallas_call(fused_kernel, out_shape=[jax.ShapeDtypeStruct(query.shape,...]
    psum x1 -> x0, blocking collectives: 45 us -> none  [shards(): lax.psum(jnp.concatenate(pieces, axis=0), 'seq').astype(jnp.bfloat16)]
    all_to_all x2 -> x0, starting transfers between devices: 11.9 us -> none  [the longest x1 7.38 us: shards(): lax.all_to_all(outgoing, 'seq', split_axis=0, concat_axis=0, tiled=True)]
    reshape x9 -> x0, local copies, waits for them, and re-layouts: 10.3 us -> none  [the longest x1 3.62 us: shards(): key_term.reshape(block_count, key_count, BLOCK_TOKENS, feature_width)]
    ppermute x4 -> x0, waiting for transfers between devices: 7.39 us -> none  [the longest x2 7.38 us: extended_2(): lax.ppermute(lax.slice_in_dim(block, block.shape[dim] - width, None, axis...]
    ppermute x4 -> x0, starting transfers between devices: 6.63 us -> none  [the longest x2 4.83 us: extended_2(): lax.ppermute(lax.slice_in_dim(block, 0, width, axis=dim), axis, backward)]
    transpose x2 -> x0, local copies, waits for them, and re-layouts: 5.35 us -> none  [the longest x1 2.67 us: shards(): jnp.einsum('bhqk,bqhd->bkhd', softmax_weights, gradient_rows, preferred_e...]
  transfers between devices with their start and end apart: 7 -> 0, of which waited for: 2 -> 0; matrix products, arithmetic and copies ran while one was open for 9% -> 0% of each run, Pallas kernels for 0% -> 0%
where the time goes in v1:
time: 53.8 us; the launch traced here: 53.6 us
  Pallas kernels  45.9 us (85%)
  local copies, waits for them, and re-layouts  7.01 us (13%)
  between operations  0.65 us (1%)
    pallas_call x1, Pallas kernels, fused(): pl.pallas_call(fused_kernel, out_shape=[jax.ShapeDtypeStruct(query.shape,...  45.9 us
    unnamed x15, local copies, waits for them, and re-layouts  7.01 us

profile of v1, /device:TPU:0, one launch (start us, length us, event | category | flops | bytes accessed | tf_op | source)
XLA Modules:
  0.0 53.6 jit_solution(4979253445964405310)
XLA Ops:
  0.6 0.0 copy-start.4
  0.6 0.8 %copy.10.rand_ref = s32[32,2]{1,0:T(8,128)S(1)} copy(s32[32,2]{0,1:T(2,128)} %param.10) | data formatting | bytes 512 | tf_op args[4]
  1.4 0.0 copy-done.4
  1.4 0.0 copy-start
  1.4 0.9 %copy-done = bf16[256,256]{1,0:T(8,128)(2,1)S(1)} copy-done((bf16[256,256]{1,0:T(8,128)(2,1)S(1)}, bf16[256,256]{1,0:T(8,128)(2,1)}, u32[]{:S(2)}) %copy-start) | copy-done | bytes 131096
  2.3 0.0 copy-start.1
  2.3 0.9 %copy-done.1 = bf16[256,256]{1,0:T(8,128)(2,1)S(1)} copy-done((bf16[256,256]{1,0:T(8,128)(2,1)S(1)}, bf16[256,256]{1,0:T(8,128)(2,1)}, u32[]{:S(2)}) %copy-start.1) | copy-done | bytes 131096
  3.2 0.0 copy-start.2
  3.2 0.9 %copy-done.2 = bf16[256,256]{1,0:T(8,128)(2,1)S(1)} copy-done((bf16[256,256]{1,0:T(8,128)(2,1)S(1)}, bf16[256,256]{1,0:T(8,128)(2,1)}, u32[]{:S(2)}) %copy-start.2) | copy-done | bytes 131096
  4.1 0.0 copy-start.3
  4.1 0.9 %copy-done.3 = bf16[256,256]{1,0:T(8,128)(2,1)S(1)} copy-done((bf16[256,256]{1,0:T(8,128)(2,1)S(1)}, bf16[256,256]{1,0:T(8,128)(2,1)}, u32[]{:S(2)}) %copy-start.3) | copy-done | bytes 131096
  5.0 45.9 %shard_map.93 = (bf16[256,256]{1,0:T(8,128)(2,1)S(1)}, bf16[256,256]{1,0:T(8,128)(2,1)S(1)}, bf16[256,256]{1,0:T(8,128)(2,1)S(1)}, bf16[256,256]{1,0:T(8,128)(2,1)S(1)}) custom-call(s32[32,2]{1,0:T(8,128)S(1)} %copy.10.rand_ref, s32[2]{0:T(128)S(1)} %copy-done.4, bf16[256,256]{1,0:T(8,128)(2,1)S(1)} %copy-done, bf16[256,256]{1,0:T(8,128)(2,1)S(1)} %copy-done.1, ...), custom_call_target="tpu_custom_call" | custom-call | flops 1610612736 | bytes 1048576 | tf_op jit(solution)/shard_map/pallas_call | solution.py:475
  51.0 0.7 %copy.15 = bf16[256,256]{1,0:T(8,128)(2,1)} copy(bf16[256,256]{1,0:T(8,128)(2,1)S(1)} %get-tuple-element.8) | data formatting | bytes 262144
  51.6 0.7 %copy.16 = bf16[256,256]{1,0:T(8,128)(2,1)} copy(bf16[256,256]{1,0:T(8,128)(2,1)S(1)} %get-tuple-element.9) | data formatting | bytes 262144
  52.3 0.7 %copy.17 = bf16[256,256]{1,0:T(8,128)(2,1)} copy(bf16[256,256]{1,0:T(8,128)(2,1)S(1)} %get-tuple-element.10) | data formatting | bytes 262144
  52.9 0.7 %copy.18 = bf16[256,256]{1,0:T(8,128)(2,1)} copy(bf16[256,256]{1,0:T(8,128)(2,1)S(1)} %get-tuple-element.11) | data formatting | bytes 262144
Async XLA Ops:
  0.6 0.8 %copy-start.4 = (s32[2]{0:T(128)S(1)}, s32[2]{0:T(128)}, u32[]{:S(2)}) copy-start(s32[2]{0:T(128)} %glob_ref.1) | copy-start | bytes 28
  1.4 0.9 %copy-start = (bf16[256,256]{1,0:T(8,128)(2,1)S(1)}, bf16[256,256]{1,0:T(8,128)(2,1)}, u32[]{:S(2)}) copy-start(bf16[256,256]{1,0:T(8,128)(2,1)} %q_ref.1) | copy-start | bytes 393220
  2.3 0.9 %copy-start.1 = (bf16[256,256]{1,0:T(8,128)(2,1)S(1)}, bf16[256,256]{1,0:T(8,128)(2,1)}, u32[]{:S(2)}) copy-start(bf16[256,256]{1,0:T(8,128)(2,1)} %k_ref.1) | copy-start | bytes 393220
  3.2 0.9 %copy-start.2 = (bf16[256,256]{1,0:T(8,128)(2,1)S(1)}, bf16[256,256]{1,0:T(8,128)(2,1)}, u32[]{:S(2)}) copy-start(bf16[256,256]{1,0:T(8,128)(2,1)} %v_ref.1) | copy-start | bytes 393220
  4.1 0.9 %copy-start.3 = (bf16[256,256]{1,0:T(8,128)(2,1)S(1)}, bf16[256,256]{1,0:T(8,128)(2,1)}, u32[]{:S(2)}) copy-start(bf16[256,256]{1,0:T(8,128)(2,1)} %g_ref.1) | copy-start | bytes 393220

commit v2 on v0

--- a/solution.py
+++ b/solution.py
@@ -3,6 +3,8 @@
 import jax
 import jax.numpy as jnp
 from jax import lax
+from jax.experimental import pallas as pl
+from jax.experimental.pallas import tpu as pltpu
 from jax.sharding import PartitionSpec as P
 
 HEAD_SIZE = 128
@@ -21,6 +23,14 @@
         high = lax.ppermute(lax.slice_in_dim(block, 0, width, axis=dim), axis, backward)
         block = jnp.concatenate([low, block, high], axis=dim)
     return block
+
+
+def pick_blocks(blocks, index):
+    onehot = (index[..., None] == jnp.arange(blocks.shape[0])).astype(blocks.dtype)
+    picked = jnp.einsum(
+        "...b,bqc->...qc", onehot, blocks, preferred_element_type=jnp.float32
+    )
+    return picked.astype(blocks.dtype)
 
 
 def shards(query, key_states, values, grad_out, rand_blocks, global_blocks):
@@ -63,15 +73,15 @@
     valid = jnp.any(matched, axis=1)
     send_local = jnp.sum(jnp.where(matched, local_table[:, :, None], 0), axis=1)
     outgoing = jnp.where(
-        valid[:, :, None, None], paired_blocks[send_local], jnp.zeros((), jnp.bfloat16)
+        valid[:, :, None, None], pick_blocks(paired_blocks, send_local), jnp.zeros((), jnp.bfloat16)
     )
     incoming = lax.all_to_all(outgoing, "seq", split_axis=0, concat_axis=0, tiled=True)
     my_owner = lax.dynamic_index_in_dim(owner_table, myself, 0, keepdims=False)
     my_rank = lax.dynamic_index_in_dim(rank_table, myself, 0, keepdims=False)
     flat_slot = my_owner * slots + my_rank
-    fetched = incoming.reshape(nshard * slots, BLOCK_TOKENS, double_width)[flat_slot].reshape(
-        block_count, nrand, BLOCK_TOKENS, double_width
-    )
+    fetched = pick_blocks(
+        incoming.reshape(nshard * slots, BLOCK_TOKENS, double_width), flat_slot
+    ).reshape(block_count, nrand, BLOCK_TOKENS, double_width)
     ext_blocks = extended.reshape(block_count + 2, BLOCK_TOKENS, double_width)
     window_blocks = jnp.stack([ext_blocks[:-2], ext_blocks[1:-1], ext_blocks[2:]], axis=1)
     glob_wide = jnp.broadcast_to(
@@ -162,7 +172,344 @@
     return (out, query_gradient, dkey, dvalue)
 
 
+PAIRS = 4
+SIDE = 2 * HEAD_SIZE
+MASKED = -1e30
+NT = (((1,), (1,)), ((), ()))
+TN = (((0,), (0,)), ((), ()))
+NN = (((1,), (0,)), ((), ()))
+
+
+def dot(a, b, dims):
+    return lax.dot_general(a, b, dims, preferred_element_type=jnp.float32)
+
+
+def fused_kernel(
+    rand_ref, glob_ref, q_ref, k_ref, v_ref, g_ref,
+    res_ref,
+    kv, own, qg, pack, bias, score, dprob, top, total, acc_out, acc_dq,
+    part, cross, cross_in, line, line_in, swap_out, swap_in,
+    loaded, line_sent, cross_sent, kv_got, swap_sent, swap_got,
+    grad_cross_sent, grad_cross_got, grad_line_sent, grad_line_got,
+):
+    tokens = q_ref.shape[0]
+    rows = 2 * tokens
+    blocks = tokens // BLOCK_TOKENS
+    nrand = rand_ref.shape[0]
+    nglob = glob_ref.shape[0]
+    block_total = rand_ref.shape[1]
+    scale = 1.0 / math.sqrt(HEAD_SIZE)
+    scale2 = scale * math.log2(math.e)
+
+    s = lax.axis_index("seq")
+    z, x = s // 2, s % 2
+    partner = s + 1 - 2 * x
+    zq = z % 2
+    mate = z + 1 - 2 * zq
+    skip = (z + 2) % PAIRS
+    mirror = PAIRS - 1 - z
+    head = ((z + 1) // 2) % 2
+    tour = (skip, mirror, mate)
+
+    def remote(src, dst, sent, got, to):
+        return pltpu.make_async_remote_copy(
+            src_ref=src, dst_ref=dst, send_sem=sent, recv_sem=got,
+            device_id={"seq": to}, device_id_type=pl.DeviceIdType.MESH,
+        )
+
+    def kv_line(zz):
+        their_head = ((zz + 1) // 2) % 2
+        return remote(own.at[their_head], kv.at[s], line_sent.at[zz], kv_got.at[s], 2 * zz + x)
+
+    def kv_cross(zz):
+        slot = 2 * zz + x
+        return remote(kv.at[slot], kv.at[slot], cross_sent.at[zz], kv_got.at[slot], partner)
+
+    def kv_arrival(slot):
+        return remote(kv.at[slot], kv.at[slot], cross_sent.at[0], kv_got.at[slot], partner)
+
+    to_mate = 2 * mate + x
+    qg_swap = remote(pack, qg.at[zq], swap_sent.at[0], swap_got.at[0], to_mate)
+    o_swap = remote(swap_out.at[0], swap_in.at[0], swap_sent.at[1], swap_got.at[1], to_mate)
+    q_swap = remote(swap_out.at[1], swap_in.at[1], swap_sent.at[2], swap_got.at[2], to_mate)
+
+    def grad_cross(zz):
+        return remote(
+            cross.at[zz], cross_in.at[zz], grad_cross_sent.at[zz], grad_cross_got.at[zz], partner
+        )
+
+    def grad_line(zz):
+        return remote(
+            line.at[zz], line_in.at[z], grad_line_sent.at[zz], grad_line_got.at[z], 2 * zz + x
+        )
+
+    def grad_arrival(zz):
+        return remote(
+            line.at[zz], line_in.at[zz], grad_line_sent.at[zz], grad_line_got.at[zz], 2 * zz + x
+        )
+
+    mine = pl.ds(pl.multiple_of(head * HEAD_SIZE, HEAD_SIZE), HEAD_SIZE)
+    theirs = pl.ds(pl.multiple_of((1 - head) * HEAD_SIZE, HEAD_SIZE), HEAD_SIZE)
+    low, high = pl.ds(0, HEAD_SIZE), pl.ds(HEAD_SIZE, HEAD_SIZE)
+    loads = []
+    for src, lanes, dst in (
+        (q_ref, theirs, pack.at[:, low]), (g_ref, theirs, pack.at[:, high]),
+        (k_ref, low, own.at[0, :, low]), (v_ref, low, own.at[0, :, high]),
+        (k_ref, high, own.at[1, :, low]), (v_ref, high, own.at[1, :, high]),
+        (k_ref, mine, kv.at[s, :, low]), (v_ref, mine, kv.at[s, :, high]),
+        (q_ref, mine, qg.at[zq, :, low]), (g_ref, mine, qg.at[zq, :, high]),
+    ):
+        loads.append(pltpu.make_async_copy(src.at[:, lanes], dst, loaded.at[len(loads)]))
+        loads[-1].start()
+
+    barrier = pltpu.get_barrier_semaphore()
+    for to in (partner, to_mate, 2 * skip + x, 2 * mirror + x):
+        pl.semaphore_signal(
+            barrier, inc=1, device_id={"seq": to}, device_id_type=pl.DeviceIdType.MESH
+        )
+    pl.semaphore_wait(barrier, 4)
+    loads[0].wait()
+    loads[1].wait()
+    qg_swap.start()
+    for load in loads[2:8]:
+        load.wait()
+    kv_cross(z).start()
+    for zz in tour:
+        kv_line(zz).start()
+
+    lane_shard = lax.broadcasted_iota(jnp.int32, (1, rows), 1) // tokens
+    lane_block = lax.broadcasted_iota(jnp.int32, (1, rows), 1) // BLOCK_TOKENS
+    base = 4 * (z // 2) + x
+    block = (base + 2 * lane_shard) * blocks + lane_block - lane_shard * blocks
+    entries = [
+        jnp.where(block == 0, block_total - 1, block - 1),
+        block,
+        jnp.where(block == block_total - 1, 0, block + 1),
+    ]
+    for j in range(nglob):
+        entries.append(jnp.full((1, rows), glob_ref[j], jnp.int32))
+    for j in range(nrand):
+        entry = jnp.zeros((1, rows), jnp.int32)
+        for i in range(2 * blocks):
+            there = (base + 2 * (i // blocks)) * blocks + i % blocks
+            entry = jnp.where(lane_block == i, rand_ref[j, there], entry)
+        entries.append(entry)
+    key_block = lax.broadcasted_iota(jnp.int32, (block_total, rows), 0)
+    count = jnp.zeros((block_total, rows), jnp.float32)
+    for entry in entries:
+        count = count + jnp.where(key_block == entry, 1.0, 0.0)
+    bias_all = jnp.where(count > 0.0, jnp.log2(jnp.maximum(count, 1.0)), MASKED)
+    for j in range(2 * PAIRS):
+        bias[j] = bias_all[j * blocks : (j + 1) * blocks]
+
+    top[...] = jnp.full_like(top, MASKED)
+    total[...] = jnp.zeros_like(total)
+    acc_out[...] = jnp.zeros_like(acc_out)
+    acc_dq[...] = jnp.zeros_like(acc_dq)
+    loads[8].wait()
+    loads[9].wait()
+    remote(pack, qg.at[1 - zq], swap_sent.at[0], swap_got.at[0], to_mate).wait_recv()
+
+    def queries():
+        return qg[:, :, :HEAD_SIZE].reshape(rows, HEAD_SIZE)
+
+    def grads():
+        return qg[:, :, HEAD_SIZE:].reshape(rows, HEAD_SIZE)
+
+    def tour_at(i):
+        return jnp.where(i == 0, skip, jnp.where(i == 1, mirror, jnp.where(i == 2, mate, z)))
+
+    def forward(slot):
+        key = kv[slot, :, :HEAD_SIZE]
+        value = kv[slot, :, HEAD_SIZE:]
+        st = dot(key, queries(), NT) * scale2
+        st = (st.reshape(blocks, BLOCK_TOKENS, rows) + bias[slot][:, None, :]).reshape(tokens, rows)
+        score[slot] = st
+        old = top[...]
+        new = jnp.maximum(old, jnp.max(st, axis=0, keepdims=True))
+        e = jnp.exp2(st - new)
+        alpha = jnp.exp2(old - new)
+        top[...] = new
+        total[...] = total[...] * alpha + jnp.sum(e, axis=0, keepdims=True)
+        acc_out[...] = acc_out[...] * alpha + dot(value, e.astype(jnp.bfloat16), TN)
+        dprob[slot] = dot(value, grads(), NT)
+
+    @pl.loop(0, 8)
+    def _(i):
+        zz = jnp.where(i < 2, z, tour_at((i - 2) % 3))
+        column = jnp.where((i == 1) | (i > 4), 1 - x, x)
+        slot = 2 * zz + column
+
+        @pl.when(i > 0)
+        def _():
+            kv_arrival(slot).wait_recv()
+
+        @pl.when((i >= 2) & (i <= 4))
+        def _():
+            kv_cross(zz).start()
+
+        forward(slot)
+
+    lse = top[...] + jnp.log2(total[...])
+    out_t = (acc_out[...] / total[...]).astype(jnp.bfloat16).astype(jnp.float32)
+    grad_t = grads().astype(jnp.float32).T
+    delta = jnp.sum(out_t * grad_t, axis=0, keepdims=True)
+    acc_out[...] = out_t
+    top[...] = lse
+    total[...] = delta
+
+    def backward(slot):
+        prob = jnp.exp2(score[slot] - top[...])
+        ds = (prob * (dprob[slot] - total[...]) * scale).astype(jnp.bfloat16)
+        dk_term = dot(ds, queries(), NN)
+        dv_term = dot(prob.astype(jnp.bfloat16), grads(), NN)
+        return ds, dk_term, dv_term
+
+    def add_dq(slot, ds):
+        acc_dq[...] += dot(kv[slot, :, :HEAD_SIZE], ds, TN)
+
+    @pl.loop(0, 4)
+    def _(i):
+        zz = tour_at(i)
+        slot = 2 * zz + 1 - x
+        ds, dk_term, dv_term = backward(slot)
+        cross[zz, :, :HEAD_SIZE] = dk_term.astype(jnp.bfloat16)
+        cross[zz, :, HEAD_SIZE:] = dv_term.astype(jnp.bfloat16)
+        grad_cross(zz).start()
+        add_dq(slot, ds)
+
+    def hand_back(which, rows_t, swap):
+        turned = rows_t.T.astype(jnp.bfloat16)
+        first, second = turned[:tokens], turned[tokens:]
+        swap_out[which] = jnp.where(zq == 0, second, first)
+        res_ref[which, :, mine] = jnp.where(zq == 0, first, second)
+        swap.start()
+
+    hand_back(0, acc_out[...], o_swap)
+
+    @pl.loop(0, 4)
+    def _(i):
+        zz = tour_at(i)
+        slot = 2 * zz + x
+        ds, dk_term, dv_term = backward(slot)
+        part[zz, :, :HEAD_SIZE] = dk_term
+        part[zz, :, HEAD_SIZE:] = dv_term
+        add_dq(slot, ds)
+
+        @pl.when(i < 3)
+        def _():
+            grad_cross(zz).wait_recv()
+            added = part[zz] + cross_in[zz].astype(jnp.float32)
+            line[zz] = added.astype(jnp.bfloat16)
+            grad_line(zz).start()
+
+    hand_back(1, acc_dq[...], q_swap)
+
+    grad_cross(z).wait_recv()
+    grad_arrival(mirror).wait_recv()
+    same = part[z] + cross_in[z].astype(jnp.float32) + line_in[mirror].astype(jnp.float32)
+    res_ref[2, :, mine] = same[:, :HEAD_SIZE].astype(jnp.bfloat16)
+    res_ref[3, :, mine] = same[:, HEAD_SIZE:].astype(jnp.bfloat16)
+
+    qg_swap.wait_send()
+    kv_cross(z).wait_send()
+    for zz in tour:
+        kv_line(zz).wait_send()
+        kv_cross(zz).wait_send()
+    o_swap.wait()
+    res_ref[0, :, theirs] = swap_in[0]
+    q_swap.wait()
+    res_ref[1, :, theirs] = swap_in[1]
+    grad_arrival(skip).wait_recv()
+    grad_arrival(mate).wait_recv()
+    other = line_in[skip].astype(jnp.float32) + line_in[mate].astype(jnp.float32)
+    res_ref[2, :, theirs] = other[:, :HEAD_SIZE].astype(jnp.bfloat16)
+    res_ref[3, :, theirs] = other[:, HEAD_SIZE:].astype(jnp.bfloat16)
+    for zz in tour:
+        grad_cross(zz).wait_send()
+        grad_line(zz).wait_send()
+    grad_cross(z).wait_send()
+
+
+def split_kernel(res_ref, o_ref, dq_ref, dk_ref, dv_ref, sems):
+    copies = [
+        pltpu.make_async_copy(res_ref.at[i], dst, sems.at[i])
+        for i, dst in enumerate((o_ref, dq_ref, dk_ref, dv_ref))
+    ]
+    for copy in copies:
+        copy.start()
+    for copy in copies:
+        copy.wait()
+
+
+def fused(query, key_states, values, grad_out, rand_blocks, global_blocks):
+    tokens = query.shape[0]
+    rows = 2 * tokens
+    slots = 2 * PAIRS
+    blocks = tokens // BLOCK_TOKENS
+    bf16, f32 = jnp.bfloat16, jnp.float32
+    vmem = pl.BlockSpec(memory_space=pltpu.VMEM)
+    smem = pl.BlockSpec(memory_space=pltpu.SMEM)
+    hbm = pl.BlockSpec(memory_space=pl.ANY)
+    dma = pltpu.SemaphoreType.DMA
+    work = 6 * 2 * rows * slots * tokens * HEAD_SIZE
+    piece = (tokens, SIDE)
+    results = pl.pallas_call(
+        fused_kernel,
+        out_shape=jax.ShapeDtypeStruct((4,) + query.shape, bf16),
+        in_specs=[smem, smem, hbm, hbm, hbm, hbm],
+        out_specs=vmem,
+        scratch_shapes=[
+            pltpu.VMEM((slots,) + piece, bf16),
+            pltpu.VMEM((2,) + piece, bf16),
+            pltpu.VMEM((2,) + piece, bf16),
+            pltpu.VMEM(piece, bf16),
+            pltpu.VMEM((slots, blocks, rows), f32),
+            pltpu.VMEM((slots, tokens, rows), f32),
+            pltpu.VMEM((slots, tokens, rows), f32),
+            pltpu.VMEM((1, rows), f32),
+            pltpu.VMEM((1, rows), f32),
+            pltpu.VMEM((HEAD_SIZE, rows), f32),
+            pltpu.VMEM((HEAD_SIZE, rows), f32),
+            pltpu.VMEM((PAIRS,) + piece, f32),
+            pltpu.VMEM((PAIRS,) + piece, bf16),
+            pltpu.VMEM((PAIRS,) + piece, bf16),
+            pltpu.VMEM((PAIRS,) + piece, bf16),
+            pltpu.VMEM((PAIRS,) + piece, bf16),
+            pltpu.VMEM((2, tokens, HEAD_SIZE), bf16),
+            pltpu.VMEM((2, tokens, HEAD_SIZE), bf16),
+            dma((10,)), dma((PAIRS,)), dma((PAIRS,)), dma((slots,)), dma((3,)), dma((3,)),
+            dma((PAIRS,)), dma((PAIRS,)), dma((PAIRS,)), dma((PAIRS,)),
+        ],
+        compiler_params=pltpu.CompilerParams(
+            collective_id=0, has_side_effects=True, vmem_limit_bytes=60 * 1024 * 1024
+        ),
+        cost_estimate=pl.CostEstimate(
+            flops=work, bytes_accessed=8 * tokens * SIDE * 2, transcendentals=2 * rows * slots * tokens
+        ),
+    )(rand_blocks.T, global_blocks, query, key_states, values, grad_out)
+    anywhere = pl.BlockSpec(memory_space=pl.ANY)
+    return pl.pallas_call(
+        split_kernel,
+        out_shape=[jax.ShapeDtypeStruct(query.shape, bf16)] * 4,
+        in_specs=[anywhere],
+        out_specs=[hbm] * 4,
+        scratch_shapes=[dma((4,))],
+        cost_estimate=pl.CostEstimate(
+            flops=0, bytes_accessed=16 * tokens * SIDE, transcendentals=0
+        ),
+    )(results)
+
+
+def device_program(query, key_states, values, grad_out, rand_blocks, global_blocks):
+    if lax.axis_size("seq") == 2 * PAIRS and query.shape == (4 * BLOCK_TOKENS, 2 * HEAD_SIZE):
+        return tuple(fused(query, key_states, values, grad_out, rand_blocks, global_blocks))
+    return shards(query, key_states, values, grad_out, rand_blocks, global_blocks)
+
+
 def solution(mesh):
     in_specs = (P("seq", "head"), P("seq", "head"), P("seq", "head"), P("seq", "head"), P(), P())
     out_specs = (P("seq", "head"), P("seq", "head"), P("seq", "head"), P("seq", "head"))
-    return jax.shard_map(shards, mesh=mesh, in_specs=in_specs, out_specs=out_specs, check_vma=False)
+    return jax.shard_map(
+        device_program, mesh=mesh, in_specs=in_specs, out_specs=out_specs, check_vma=False
+    )

time: 202 us -> 59.8 us (0.30)
  waiting for transfers between devices: 67 us -> 0 us
  Pallas kernels: 0 us -> 59 us
  blocking collectives: 45 us -> 0 us
  local copies, waits for them, and re-layouts: 37.5 us -> 0 us
  starting transfers between devices: 18.8 us -> 0 us
  between operations: 17.1 us -> 0.64 us
  other arithmetic: 10.5 us -> 0 us
  matrix products: 5.15 us -> 0 us
    psum x1 -> x0, waiting for transfers between devices: 59.6 us -> none  [shards(): glob_total = lax.psum(glob_terms, 'seq')]
    pallas_call x0 -> x2, Pallas kernels: none -> 59 us  [the longest x1 42 us: fused(): pl.pallas_call(fused_kernel, out_shape=jax.ShapeDtypeStruct((4,) + query....]
    psum x1 -> x0, blocking collectives: 45 us -> none  [shards(): lax.psum(jnp.concatenate(pieces, axis=0), 'seq').astype(jnp.bfloat16)]
    all_to_all x2 -> x0, starting transfers between devices: 11.9 us -> none  [the longest x1 7.38 us: shards(): lax.all_to_all(outgoing, 'seq', split_axis=0, concat_axis=0, tiled=True)]
    reshape x9 -> x0, local copies, waits for them, and re-layouts: 10.3 us -> none  [the longest x1 3.62 us: shards(): key_term.reshape(block_count, key_count, BLOCK_TOKENS, feature_width)]
    unnamed x30 -> x0, local copies, waits for them, and re-layouts: 8.83 us -> none
    ppermute x4 -> x0, waiting for transfers between devices: 7.39 us -> none  [the longest x2 7.38 us: extended_2(): lax.ppermute(lax.slice_in_dim(block, block.shape[dim] - width, None, axis...]
    ppermute x4 -> x0, starting transfers between devices: 6.63 us -> none  [the longest x2 4.83 us: extended_2(): lax.ppermute(lax.slice_in_dim(block, 0, width, axis=dim), axis, backward)]
  transfers between devices with their start and end apart: 7 -> 0, of which waited for: 2 -> 0; matrix products, arithmetic and copies ran while one was open for 9% -> 0% of each run, Pallas kernels for 0% -> 0%
where the time goes in v2:
time: 59.8 us; the launch traced here: 59.6 us
  Pallas kernels  59 us (99%)
  between operations  0.64 us (1%)
    pallas_call x1, Pallas kernels, fused(): pl.pallas_call(fused_kernel, out_shape=jax.ShapeDtypeStruct((4,) + query....  42 us
    pallas_call x1, Pallas kernels, fused(): pl.pallas_call(split_kernel, out_shape=[jax.ShapeDtypeStruct(query.shape,...  17 us

profile of v2, /device:TPU:0, one launch (start us, length us, event | category | flops | bytes accessed | tf_op | source)
XLA Modules:
  0.0 59.6 jit_solution(7084065867502733156)
XLA Ops:
  0.6 42.0 %shard_map.93.res_ref = bf16[4,256,256]{2,1,0:T(8,128)(2,1)} custom-call(s32[2,32]{1,0:T(2,128)} %bitcast.1, s32[2]{0:T(128)} %glob_ref.1, bf16[256,256]{1,0:T(8,128)(2,1)} %q_ref.1, bf16[256,256]{1,0:T(8,128)(2,1)} %k_ref.1, bf16[256,256]{1,0:T(8,128)(2,1)} %v_ref.1, bf16[256,256]{1,0:T(8,128)(2,1)} %g_ref.1), custom_call_target="tpu_custom_call" | custom-call | flops 1610612736 | bytes 1048576 | tf_op jit(solution)/shard_map/pallas_call | solution.py:457
  42.6 17.0 %shard_map.94 = (bf16[256,256]{1,0:T(8,128)(2,1)}, bf16[256,256]{1,0:T(8,128)(2,1)}, bf16[256,256]{1,0:T(8,128)(2,1)}, bf16[256,256]{1,0:T(8,128)(2,1)}) custom-call(bf16[4,256,256]{2,1,0:T(8,128)(2,1)} %shard_map.93.res_ref), custom_call_target="tpu_custom_call" | custom-call | bytes 1048576 | tf_op jit(solution)/shard_map/pallas_call | solution.py:492

commit v3 on v2

--- a/solution.py
+++ b/solution.py
@@ -431,15 +431,21 @@
     grad_cross(z).wait_send()
 
 
-def split_kernel(res_ref, o_ref, dq_ref, dk_ref, dv_ref, sems):
-    copies = [
-        pltpu.make_async_copy(res_ref.at[i], dst, sems.at[i])
+def split_kernel(res_ref, o_ref, dq_ref, dk_ref, dv_ref, held, sems):
+    loads = [
+        pltpu.make_async_copy(res_ref.at[i], held.at[i], sems.at[i]) for i in range(4)
+    ]
+    stores = [
+        pltpu.make_async_copy(held.at[i], dst, sems.at[4 + i])
         for i, dst in enumerate((o_ref, dq_ref, dk_ref, dv_ref))
     ]
-    for copy in copies:
-        copy.start()
-    for copy in copies:
-        copy.wait()
+    for load in loads:
+        load.start()
+    for load, store in zip(loads, stores):
+        load.wait()
+        store.start()
+    for store in stores:
+        store.wait()
 
 
 def fused(query, key_states, values, grad_out, rand_blocks, global_blocks):
@@ -494,7 +500,7 @@
         out_shape=[jax.ShapeDtypeStruct(query.shape, bf16)] * 4,
         in_specs=[anywhere],
         out_specs=[hbm] * 4,
-        scratch_shapes=[dma((4,))],
+        scratch_shapes=[pltpu.VMEM((4,) + query.shape, bf16), dma((8,))],
         cost_estimate=pl.CostEstimate(
             flops=0, bytes_accessed=16 * tokens * SIDE, transcendentals=0
         ),

time: 59.8 us -> 44.6 us (0.75)
  Pallas kernels: 59 us -> 43.8 us
    pallas_call x1, Pallas kernels: 17 us -> 1.82 us  [fused(): pl.pallas_call(split_kernel, out_shape=[jax.ShapeDtypeStruct(query.shape,...]
where the time goes in v3:
time: 44.6 us; the launch traced here: 44.4 us
  Pallas kernels  43.8 us (98%)
  between operations  0.64 us (1%)
    pallas_call x1, Pallas kernels, fused(): pl.pallas_call(fused_kernel, out_shape=jax.ShapeDtypeStruct((4,) + query....  42 us
    pallas_call x1, Pallas kernels, fused(): pl.pallas_call(split_kernel, out_shape=[jax.ShapeDtypeStruct(query.shape,...  1.82 us

profile of v3, /device:TPU:0, one launch (start us, length us, event | category | flops | bytes accessed | tf_op | source)
XLA Modules:
  0.0 44.4 jit_solution(18117585796775289470)
XLA Ops:
  0.6 42.0 %shard_map.93.res_ref = bf16[4,256,256]{2,1,0:T(8,128)(2,1)} custom-call(s32[2,32]{1,0:T(2,128)} %bitcast.1, s32[2]{0:T(128)} %glob_ref.1, bf16[256,256]{1,0:T(8,128)(2,1)} %q_ref.1, bf16[256,256]{1,0:T(8,128)(2,1)} %k_ref.1, bf16[256,256]{1,0:T(8,128)(2,1)} %v_ref.1, bf16[256,256]{1,0:T(8,128)(2,1)} %g_ref.1), custom_call_target="tpu_custom_call" | custom-call | flops 1610612736 | bytes 1048576 | tf_op jit(solution)/shard_map/pallas_call | solution.py:463
  42.6 1.8 %shard_map.94 = (bf16[256,256]{1,0:T(8,128)(2,1)}, bf16[256,256]{1,0:T(8,128)(2,1)}, bf16[256,256]{1,0:T(8,128)(2,1)}, bf16[256,256]{1,0:T(8,128)(2,1)}) custom-call(bf16[4,256,256]{2,1,0:T(8,128)(2,1)} %shard_map.93.res_ref), custom_call_target="tpu_custom_call" | custom-call | bytes 1048576 | tf_op jit(solution)/shard_map/pallas_call | solution.py:498

commit v4 on v3

--- a/solution.py
+++ b/solution.py
@@ -210,6 +210,10 @@
     mirror = PAIRS - 1 - z
     head = ((z + 1) // 2) % 2
     tour = (skip, mirror, mate)
+    end = head == 0
+    out_order = (jnp.where(end, skip, mirror), jnp.where(end, mirror, mate), jnp.where(end, mate, skip))
+    in_order = (jnp.where(end, mate, mirror), jnp.where(end, mirror, skip), jnp.where(end, skip, mate))
+    back_order = (jnp.where(end, skip, mate), jnp.where(end, mirror, skip), jnp.where(end, mate, mirror))
 
     def remote(src, dst, sent, got, to):
         return pltpu.make_async_remote_copy(
@@ -274,7 +278,7 @@
     for load in loads[2:8]:
         load.wait()
     kv_cross(z).start()
-    for zz in tour:
+    for zz in out_order:
         kv_line(zz).start()
 
     lane_shard = lax.broadcasted_iota(jnp.int32, (1, rows), 1) // tokens
@@ -317,7 +321,10 @@
         return qg[:, :, HEAD_SIZE:].reshape(rows, HEAD_SIZE)
 
     def tour_at(i):
-        return jnp.where(i == 0, skip, jnp.where(i == 1, mirror, jnp.where(i == 2, mate, z)))
+        return pick(back_order, i)
+
+    def pick(order, i):
+        return jnp.where(i == 0, order[0], jnp.where(i == 1, order[1], jnp.where(i == 2, order[2], z)))
 
     def forward(slot):
         key = kv[slot, :, :HEAD_SIZE]
@@ -336,7 +343,8 @@
 
     @pl.loop(0, 8)
     def _(i):
-        zz = jnp.where(i < 2, z, tour_at((i - 2) % 3))
+        at = (i - 2) % 3
+        zz = jnp.where(i < 2, z, pick(in_order, at))
         column = jnp.where((i == 1) | (i > 4), 1 - x, x)
         slot = 2 * zz + column
 
@@ -368,16 +376,6 @@
     def add_dq(slot, ds):
         acc_dq[...] += dot(kv[slot, :, :HEAD_SIZE], ds, TN)
 
-    @pl.loop(0, 4)
-    def _(i):
-        zz = tour_at(i)
-        slot = 2 * zz + 1 - x
-        ds, dk_term, dv_term = backward(slot)
-        cross[zz, :, :HEAD_SIZE] = dk_term.astype(jnp.bfloat16)
-        cross[zz, :, HEAD_SIZE:] = dv_term.astype(jnp.bfloat16)
-        grad_cross(zz).start()
-        add_dq(slot, ds)
-
     def hand_back(which, rows_t, swap):
         turned = rows_t.T.astype(jnp.bfloat16)
         first, second = turned[:tokens], turned[tokens:]
@@ -385,23 +383,35 @@
         res_ref[which, :, mine] = jnp.where(zq == 0, first, second)
         swap.start()
 
-    hand_back(0, acc_out[...], o_swap)
-
     @pl.loop(0, 4)
     def _(i):
         zz = tour_at(i)
+        before = tour_at(i - 1)
+        slot = 2 * zz + 1 - x
+        ds, dk_term, dv_term = backward(slot)
+        cross[zz, :, :HEAD_SIZE] = dk_term.astype(jnp.bfloat16)
+        cross[zz, :, HEAD_SIZE:] = dv_term.astype(jnp.bfloat16)
+
+        grad_cross(zz).start()
+        add_dq(slot, ds)
+
+        @pl.when(i == 0)
+        def _():
+            hand_back(0, acc_out[...], o_swap)
+
         slot = 2 * zz + x
         ds, dk_term, dv_term = backward(slot)
         part[zz, :, :HEAD_SIZE] = dk_term
         part[zz, :, HEAD_SIZE:] = dv_term
         add_dq(slot, ds)
 
-        @pl.when(i < 3)
+        @pl.when(i > 0)
         def _():
-            grad_cross(zz).wait_recv()
-            added = part[zz] + cross_in[zz].astype(jnp.float32)
-            line[zz] = added.astype(jnp.bfloat16)
-            grad_line(zz).start()
+            grad_cross(before).wait_recv()
+            added = part[before] + cross_in[before].astype(jnp.float32)
+            line[before] = added.astype(jnp.bfloat16)
+
+            grad_line(before).start()
 
     hand_back(1, acc_dq[...], q_swap)
 
@@ -411,10 +421,11 @@
     res_ref[2, :, mine] = same[:, :HEAD_SIZE].astype(jnp.bfloat16)
     res_ref[3, :, mine] = same[:, HEAD_SIZE:].astype(jnp.bfloat16)
 
+    kv_cross(z).wait_send()
     qg_swap.wait_send()
-    kv_cross(z).wait_send()
     for zz in tour:
         kv_line(zz).wait_send()
+    for zz in tour:
         kv_cross(zz).wait_send()
     o_swap.wait()
     res_ref[0, :, theirs] = swap_in[0]

time: 44.6 us -> 43.3 us (0.971)
  Pallas kernels: 43.8 us -> 42.5 us
    pallas_call x1, Pallas kernels: 42 us -> 40.6 us  [fused(): pl.pallas_call(fused_kernel, out_shape=jax.ShapeDtypeStruct((4,) + query....]
where the time goes in v4:
time: 43.3 us; the launch traced here: 43.1 us
  Pallas kernels  42.5 us (98%)
  between operations  0.64 us (1%)
    pallas_call x1, Pallas kernels, fused(): pl.pallas_call(fused_kernel, out_shape=jax.ShapeDtypeStruct((4,) + query....  40.6 us
    pallas_call x1, Pallas kernels, fused(): pl.pallas_call(split_kernel, out_shape=[jax.ShapeDtypeStruct(query.shape,...  1.82 us

profile of v4, /device:TPU:0, one launch (start us, length us, event | category | flops | bytes accessed | tf_op | source)
XLA Modules:
  0.0 43.1 jit_solution(5630048839659804431)
XLA Ops:
  0.6 40.6 %shard_map.93.res_ref = bf16[4,256,256]{2,1,0:T(8,128)(2,1)} custom-call(s32[2,32]{1,0:T(2,128)} %bitcast.1, s32[2]{0:T(128)} %glob_ref.1, bf16[256,256]{1,0:T(8,128)(2,1)} %q_ref.1, bf16[256,256]{1,0:T(8,128)(2,1)} %k_ref.1, bf16[256,256]{1,0:T(8,128)(2,1)} %v_ref.1, bf16[256,256]{1,0:T(8,128)(2,1)} %g_ref.1), custom_call_target="tpu_custom_call" | custom-call | flops 1610612736 | bytes 1048576 | tf_op jit(solution)/shard_map/pallas_call | solution.py:474
  41.3 1.8 %shard_map.94 = (bf16[256,256]{1,0:T(8,128)(2,1)}, bf16[256,256]{1,0:T(8,128)(2,1)}, bf16[256,256]{1,0:T(8,128)(2,1)}, bf16[256,256]{1,0:T(8,128)(2,1)}) custom-call(bf16[4,256,256]{2,1,0:T(8,128)(2,1)} %shard_map.93.res_ref), custom_call_target="tpu_custom_call" | custom-call | bytes 1048576 | tf_op jit(solution)/shard_map/pallas_call | solution.py:509
